TPU v7x, 128 devices: a whole 4x4x4 slice. The times are simulated.
128 devices in a mesh: tm: 16 (over z_hi, y, core), tensor: 8 (over x, z_lo).
Axes of the slice: x: 4, y: 4, z: 4 (z_hi: 2, z_lo: 2; z = z_hi * 2 + z_lo), core: 2. Of those that a mesh axis runs over, the one named last changes fastest.
Arguments:
- queries: bfloat16 [1024, 5120], P('tm', 'tensor'), may hold values from -150 to 150
- cached_keys: bfloat16 [65536, 5120], P('tm', 'tensor'), may hold values from -20 to 20
- cached_values: bfloat16 [65536, 5120], P('tm', 'tensor'), may hold values from -6 to 6
- out_weight: bfloat16 [5120, 5120], P('tensor'), may hold values from -0.078125 to 0.078125
Outputs:
- united: float32 [1024, 5120], P('tm', 'tensor')
All inputs are finite; a program needn't handle non-finite values.
Results may differ from a plain program's by a relative error of at most 0.0044.
Values may be sent and summed in bfloat16 or wider, within the bound.
A program may use at most 128 MiB of HBM per device.

v0:
```python
import math

import jax
import jax.numpy as jnp
from jax import lax
from jax.sharding import PartitionSpec as P

HD = 128


def shifted(block, axis, distance):
    devices = range(lax.axis_size(axis))
    route = [((i - distance) % len(devices), i) for i in devices]
    return lax.ppermute(block, axis, route)


def fresh_state(head_count, row_count):
    running = jnp.full((head_count, row_count), -jnp.inf, jnp.float32)
    totals = jnp.zeros((head_count, row_count), jnp.float32)
    accumulated = jnp.zeros((head_count, row_count, HD), jnp.float32)
    return (running, totals, accumulated)


def attend(queries, cached_keys, cached_values, carried):
    row_count = queries.shape[0]
    key_count = cached_keys.shape[0]
    head_count = cached_keys.shape[1] // HD
    scaling = 1.0 / math.sqrt(HD)
    query_heads = queries.reshape(row_count, head_count, HD)
    key_heads = cached_keys.reshape(key_count, head_count, HD)
    value_heads = cached_values.reshape(key_count, head_count, HD)
    block_size = min(512, key_count)
    block_count = key_count // block_size

    def block_step(carried_state, block_index):
        running, totals, accumulated = carried_state
        key_block = lax.dynamic_slice_in_dim(key_heads, block_index * block_size, block_size, 0)
        value_block = lax.dynamic_slice_in_dim(
            value_heads, block_index * block_size, block_size, 0
        ).astype(jnp.float32)
        scores = (
            jnp.einsum("rhd,khd->hrk", query_heads, key_block, preferred_element_type=jnp.float32)
            * scaling
        )
        new_top = jnp.maximum(running, jnp.max(scores, axis=2))
        factor = jnp.exp(running - new_top)
        probs = jnp.exp(scores - new_top[:, :, None])
        totals = totals * factor + jnp.sum(probs, axis=2)
        accumulated = accumulated * factor[:, :, None] + jnp.einsum(
            "hrk,khd->hrd", probs, value_block, precision=lax.Precision.HIGHEST
        )
        return ((new_top, totals, accumulated), None)

    final_state, _ = lax.scan(block_step, carried, jnp.arange(block_count, dtype=jnp.int32))
    return final_state


def normalize(carried):
    running, totals, accumulated = carried
    head_count, row_count = totals.shape
    attended = accumulated / totals[:, :, None]
    return (
        jnp.transpose(attended, (1, 0, 2)).reshape(row_count, head_count * HD).astype(jnp.bfloat16)
    )


def on_device(queries, cached_keys, cached_values, out_weight):
    members = lax.axis_size("tm")
    row_count = queries.shape[0]
    head_count = queries.shape[1] // HD
    carried = attend(queries, cached_keys, cached_values, fresh_state(head_count, row_count))

    def travel(turn, loop_state):
        moving, carried_state = loop_state
        moving = shifted(moving, "tm", 1)
        carried_state = shifted(carried_state, "tm", 1)
        return (moving, attend(moving, cached_keys, cached_values, carried_state))

    moving, carried = lax.fori_loop(0, members - 1, travel, (queries, carried))
    mixed_heads = shifted(normalize(carried), "tm", 1)
    partial_out = jnp.dot(mixed_heads, out_weight, preferred_element_type=jnp.float32)
    return lax.psum_scatter(partial_out, "tensor", scatter_dimension=1, tiled=True)


def solution(mesh):
    placed = (P("tm", "tensor"), P("tm", "tensor"), P("tm", "tensor"), P("tensor", None))
    return jax.shard_map(
        on_device, mesh=mesh, in_specs=placed, out_specs=P("tm", "tensor"), check_vma=False
    )
```

profile of v0, /device:TPU:0, one launch (start us, length us, event | category | flops | bytes accessed | tf_op | source)
XLA Modules:
  0.0 837.0 jit_solution(4248843288505294004)
XLA Ops:
  7.4 7.9 copy.9
  15.4 8.0 copy.10
  23.4 39.8 %while.47 = (s32[]{:T(128)}, f32[5,64]{1,0:T(8,128)S(1)}, f32[5,64]{1,0:T(8,128)S(1)}, f32[5,64,128]{2,1,0:T(8,128)S(1)}, s32[8]{0:T(128)S(1)}, /*index=5*/bf16[...) while((s32[]{:T(128)}, f32[5,64]{1,0:T(8,128)S(1)}, ...), condition=%wide.region_3.4_spmd.clone, body=%wide.region_0.3_spmd.clone.sunk | while | flops 294544960 | bytes 3707075 | solution.py:54
  63.1 713.2 %while.46 = (s32[]{:T(128)}, bf16[64,640]{1,0:T(8,128)(2,1)S(1)}, f32[5,64]{1,0:T(8,128)S(1)}, f32[5,64]{1,0:T(8,128)S(1)}, f32[5,64,128]{2,1,0:T(8,128)S(1)}, /...) while((s32[]{:T(128)}, bf16[64,640]{1,0:T(8,128)(2,1)S(1)}, ...), condition=%wide.region_9.10_spmd, body=%wide.region_4.9_spmd.sunk | while | flops 294503040 | bytes 5361244 | solution.py:79
  73.0 38.0 %while.48 = (s32[]{:T(128)}, f32[5,64]{1,0:T(8,128)S(1)}, f32[5,64]{1,0:T(8,128)S(1)}, f32[5,64,128]{2,1,0:T(8,128)S(1)}, s32[8]{0:T(128)S(1)}, /*index=5*/bf16[...) while((s32[]{:T(128)}, f32[5,64]{1,0:T(8,128)S(1)}, ...), condition=%wide.region_8.8_spmd, body=%wide.region_5.7_spmd.sunk | while | flops 294503040 | bytes 3707063 | solution.py:54
  111.5 7.2 collective-permute-done
  120.5 38.0 %while.48 = (s32[]{:T(128)}, f32[5,64]{1,0:T(8,128)S(1)}, f32[5,64]{1,0:T(8,128)S(1)}, f32[5,64,128]{2,1,0:T(8,128)S(1)}, s32[8]{0:T(128)S(1)}, /*index=5*/bf16[...) while((s32[]{:T(128)}, f32[5,64]{1,0:T(8,128)S(1)}, ...), condition=%wide.region_8.8_spmd, body=%wide.region_5.7_spmd.sunk | while | flops 294503040 | bytes 3707063 | solution.py:54
  159.0 7.2 collective-permute-done
  168.1 38.0 %while.48 = (s32[]{:T(128)}, f32[5,64]{1,0:T(8,128)S(1)}, f32[5,64]{1,0:T(8,128)S(1)}, f32[5,64,128]{2,1,0:T(8,128)S(1)}, s32[8]{0:T(128)S(1)}, /*index=5*/bf16[...) while((s32[]{:T(128)}, f32[5,64]{1,0:T(8,128)S(1)}, ...), condition=%wide.region_8.8_spmd, body=%wide.region_5.7_spmd.sunk | while | flops 294503040 | bytes 3707063 | solution.py:54
  215.6 38.0 %while.48 = (s32[]{:T(128)}, f32[5,64]{1,0:T(8,128)S(1)}, f32[5,64]{1,0:T(8,128)S(1)}, f32[5,64,128]{2,1,0:T(8,128)S(1)}, s32[8]{0:T(128)S(1)}, /*index=5*/bf16[...) while((s32[]{:T(128)}, f32[5,64]{1,0:T(8,128)S(1)}, ...), condition=%wide.region_8.8_spmd, body=%wide.region_5.7_spmd.sunk | while | flops 294503040 | bytes 3707063 | solution.py:54
  263.1 38.0 %while.48 = (s32[]{:T(128)}, f32[5,64]{1,0:T(8,128)S(1)}, f32[5,64]{1,0:T(8,128)S(1)}, f32[5,64,128]{2,1,0:T(8,128)S(1)}, s32[8]{0:T(128)S(1)}, /*index=5*/bf16[...) while((s32[]{:T(128)}, f32[5,64]{1,0:T(8,128)S(1)}, ...), condition=%wide.region_8.8_spmd, body=%wide.region_5.7_spmd.sunk | while | flops 294503040 | bytes 3707063 | solution.py:54
  310.6 38.0 %while.48 = (s32[]{:T(128)}, f32[5,64]{1,0:T(8,128)S(1)}, f32[5,64]{1,0:T(8,128)S(1)}, f32[5,64,128]{2,1,0:T(8,128)S(1)}, s32[8]{0:T(128)S(1)}, /*index=5*/bf16[...) while((s32[]{:T(128)}, f32[5,64]{1,0:T(8,128)S(1)}, ...), condition=%wide.region_8.8_spmd, body=%wide.region_5.7_spmd.sunk | while | flops 294503040 | bytes 3707063 | solution.py:54
  358.1 38.0 %while.48 = (s32[]{:T(128)}, f32[5,64]{1,0:T(8,128)S(1)}, f32[5,64]{1,0:T(8,128)S(1)}, f32[5,64,128]{2,1,0:T(8,128)S(1)}, s32[8]{0:T(128)S(1)}, /*index=5*/bf16[...) while((s32[]{:T(128)}, f32[5,64]{1,0:T(8,128)S(1)}, ...), condition=%wide.region_8.8_spmd, body=%wide.region_5.7_spmd.sunk | while | flops 294503040 | bytes 3707063 | solution.py:54
  405.6 38.0 %while.48 = (s32[]{:T(128)}, f32[5,64]{1,0:T(8,128)S(1)}, f32[5,64]{1,0:T(8,128)S(1)}, f32[5,64,128]{2,1,0:T(8,128)S(1)}, s32[8]{0:T(128)S(1)}, /*index=5*/bf16[...) while((s32[]{:T(128)}, f32[5,64]{1,0:T(8,128)S(1)}, ...), condition=%wide.region_8.8_spmd, body=%wide.region_5.7_spmd.sunk | while | flops 294503040 | bytes 3707063 | solution.py:54
  453.1 38.0 %while.48 = (s32[]{:T(128)}, f32[5,64]{1,0:T(8,128)S(1)}, f32[5,64]{1,0:T(8,128)S(1)}, f32[5,64,128]{2,1,0:T(8,128)S(1)}, s32[8]{0:T(128)S(1)}, /*index=5*/bf16[...) while((s32[]{:T(128)}, f32[5,64]{1,0:T(8,128)S(1)}, ...), condition=%wide.region_8.8_spmd, body=%wide.region_5.7_spmd.sunk | while | flops 294503040 | bytes 3707063 | solution.py:54
  500.6 38.0 %while.48 = (s32[]{:T(128)}, f32[5,64]{1,0:T(8,128)S(1)}, f32[5,64]{1,0:T(8,128)S(1)}, f32[5,64,128]{2,1,0:T(8,128)S(1)}, s32[8]{0:T(128)S(1)}, /*index=5*/bf16[...) while((s32[]{:T(128)}, f32[5,64]{1,0:T(8,128)S(1)}, ...), condition=%wide.region_8.8_spmd, body=%wide.region_5.7_spmd.sunk | while | flops 294503040 | bytes 3707063 | solution.py:54
  548.1 38.0 %while.48 = (s32[]{:T(128)}, f32[5,64]{1,0:T(8,128)S(1)}, f32[5,64]{1,0:T(8,128)S(1)}, f32[5,64,128]{2,1,0:T(8,128)S(1)}, s32[8]{0:T(128)S(1)}, /*index=5*/bf16[...) while((s32[]{:T(128)}, f32[5,64]{1,0:T(8,128)S(1)}, ...), condition=%wide.region_8.8_spmd, body=%wide.region_5.7_spmd.sunk | while | flops 294503040 | bytes 3707063 | solution.py:54
  586.6 7.2 collective-permute-done
  595.7 38.0 %while.48 = (s32[]{:T(128)}, f32[5,64]{1,0:T(8,128)S(1)}, f32[5,64]{1,0:T(8,128)S(1)}, f32[5,64,128]{2,1,0:T(8,128)S(1)}, s32[8]{0:T(128)S(1)}, /*index=5*/bf16[...) while((s32[]{:T(128)}, f32[5,64]{1,0:T(8,128)S(1)}, ...), condition=%wide.region_8.8_spmd, body=%wide.region_5.7_spmd.sunk | while | flops 294503040 | bytes 3707063 | solution.py:54
  643.2 38.0 %while.48 = (s32[]{:T(128)}, f32[5,64]{1,0:T(8,128)S(1)}, f32[5,64]{1,0:T(8,128)S(1)}, f32[5,64,128]{2,1,0:T(8,128)S(1)}, s32[8]{0:T(128)S(1)}, /*index=5*/bf16[...) while((s32[]{:T(128)}, f32[5,64]{1,0:T(8,128)S(1)}, ...), condition=%wide.region_8.8_spmd, body=%wide.region_5.7_spmd.sunk | while | flops 294503040 | bytes 3707063 | solution.py:54
  690.7 38.0 %while.48 = (s32[]{:T(128)}, f32[5,64]{1,0:T(8,128)S(1)}, f32[5,64]{1,0:T(8,128)S(1)}, f32[5,64,128]{2,1,0:T(8,128)S(1)}, s32[8]{0:T(128)S(1)}, /*index=5*/bf16[...) while((s32[]{:T(128)}, f32[5,64]{1,0:T(8,128)S(1)}, ...), condition=%wide.region_8.8_spmd, body=%wide.region_5.7_spmd.sunk | while | flops 294503040 | bytes 3707063 | solution.py:54
  738.2 38.0 %while.48 = (s32[]{:T(128)}, f32[5,64]{1,0:T(8,128)S(1)}, f32[5,64]{1,0:T(8,128)S(1)}, f32[5,64,128]{2,1,0:T(8,128)S(1)}, s32[8]{0:T(128)S(1)}, /*index=5*/bf16[...) while((s32[]{:T(128)}, f32[5,64]{1,0:T(8,128)S(1)}, ...), condition=%wide.region_8.8_spmd, body=%wide.region_5.7_spmd.sunk | while | flops 294503040 | bytes 3707063 | solution.py:54
  776.5 7.5 collective-permute-done.4
  789.2 41.0 %reduce-scatter.2.cloned.1.call-done = f32[64,640]{1,0:T(8,128)} async-done(((f32[64,5120]{1,0:T(8,128)}), f32[64,640]{1,0:T(8,128)}) %reduce-scatter.2.cloned.1.call-update) | async-done | bytes 163856 | tf_op jit(solution)/shard_map/reduce_scatter | solution.py:82
  (1114 shorter events, 658.9 us)
Async XLA Ops:
  6.5 823.6 %reduce-scatter.2.cloned.1.call-start = ((), (), s32[]{:S(2)}) async-start(), calls=%async_computation.1 | async-start | bytes 1474560 | tf_op jit(solution)/shard_map/reduce_scatter | solution.py:82
  63.2 9.8 %collective-permute-start.3 = (f32[5,64,128]{2,1,0:T(8,128)S(1)}, f32[5,64,128]{2,1,0:T(8,128)S(1)}, u32[]{:S(2)}, u32[]{:S(2)}) collective-permute-start(f32[5,64,128]{2,1,0:T(8,128)S(1)} %get-tuple-element.517), channel_id=1, source_target_pairs={{120,0},{0,8},{8,16},{16,24},{24,32},{32,40},{40,48},{48,56},{56,6... | collective-permute-start | bytes 491528 | tf_op jit(solution)/shard_map/while/body/eval_jaxpr/ppermute | solution.py:14
  111.2 9.3 %collective-permute-start.3 = (f32[5,64,128]{2,1,0:T(8,128)S(1)}, f32[5,64,128]{2,1,0:T(8,128)S(1)}, u32[]{:S(2)}, u32[]{:S(2)}) collective-permute-start(f32[5,64,128]{2,1,0:T(8,128)S(1)} %get-tuple-element.517), channel_id=1, source_target_pairs={{120,0},{0,8},{8,16},{16,24},{24,32},{32,40},{40,48},{48,56},{56,6... | collective-permute-start | bytes 491528 | tf_op jit(solution)/shard_map/while/body/eval_jaxpr/ppermute | solution.py:14
  111.3 9.2 %collective-permute-start.1 = (f32[5,64]{1,0:T(8,128)S(1)}, f32[5,64]{1,0:T(8,128)S(1)}, u32[]{:S(2)}, u32[]{:S(2)}) collective-permute-start(f32[5,64]{1,0:T(8,128)S(1)} %get-tuple-element.515), channel_id=1, source_target_pairs={{120,0},{0,8},{8,16},{16,24},{24,32},{32,40},{40,48},{48,56},{56,6... | collective-permute-start | bytes 3848 | tf_op jit(solution)/shard_map/while/body/eval_jaxpr/ppermute | solution.py:14
  158.7 9.3 %collective-permute-start.3 = (f32[5,64,128]{2,1,0:T(8,128)S(1)}, f32[5,64,128]{2,1,0:T(8,128)S(1)}, u32[]{:S(2)}, u32[]{:S(2)}) collective-permute-start(f32[5,64,128]{2,1,0:T(8,128)S(1)} %get-tuple-element.517), channel_id=1, source_target_pairs={{120,0},{0,8},{8,16},{16,24},{24,32},{32,40},{40,48},{48,56},{56,6... | collective-permute-start | bytes 491528 | tf_op jit(solution)/shard_map/while/body/eval_jaxpr/ppermute | solution.py:14
  158.8 9.2 %collective-permute-start.1 = (f32[5,64]{1,0:T(8,128)S(1)}, f32[5,64]{1,0:T(8,128)S(1)}, u32[]{:S(2)}, u32[]{:S(2)}) collective-permute-start(f32[5,64]{1,0:T(8,128)S(1)} %get-tuple-element.515), channel_id=1, source_target_pairs={{120,0},{0,8},{8,16},{16,24},{24,32},{32,40},{40,48},{48,56},{56,6... | collective-permute-start | bytes 3848 | tf_op jit(solution)/shard_map/while/body/eval_jaxpr/ppermute | solution.py:14
  206.2 9.3 %collective-permute-start.3 = (f32[5,64,128]{2,1,0:T(8,128)S(1)}, f32[5,64,128]{2,1,0:T(8,128)S(1)}, u32[]{:S(2)}, u32[]{:S(2)}) collective-permute-start(f32[5,64,128]{2,1,0:T(8,128)S(1)} %get-tuple-element.517), channel_id=1, source_target_pairs={{120,0},{0,8},{8,16},{16,24},{24,32},{32,40},{40,48},{48,56},{56,6... | collective-permute-start | bytes 491528 | tf_op jit(solution)/shard_map/while/body/eval_jaxpr/ppermute | solution.py:14
  206.3 9.2 %collective-permute-start.1 = (f32[5,64]{1,0:T(8,128)S(1)}, f32[5,64]{1,0:T(8,128)S(1)}, u32[]{:S(2)}, u32[]{:S(2)}) collective-permute-start(f32[5,64]{1,0:T(8,128)S(1)} %get-tuple-element.515), channel_id=1, source_target_pairs={{120,0},{0,8},{8,16},{16,24},{24,32},{32,40},{40,48},{48,56},{56,6... | collective-permute-start | bytes 3848 | tf_op jit(solution)/shard_map/while/body/eval_jaxpr/ppermute | solution.py:14
  253.8 9.3 %collective-permute-start.3 = (f32[5,64,128]{2,1,0:T(8,128)S(1)}, f32[5,64,128]{2,1,0:T(8,128)S(1)}, u32[]{:S(2)}, u32[]{:S(2)}) collective-permute-start(f32[5,64,128]{2,1,0:T(8,128)S(1)} %get-tuple-element.517), channel_id=1, source_target_pairs={{120,0},{0,8},{8,16},{16,24},{24,32},{32,40},{40,48},{48,56},{56,6... | collective-permute-start | bytes 491528 | tf_op jit(solution)/shard_map/while/body/eval_jaxpr/ppermute | solution.py:14
  253.8 9.2 %collective-permute-start.1 = (f32[5,64]{1,0:T(8,128)S(1)}, f32[5,64]{1,0:T(8,128)S(1)}, u32[]{:S(2)}, u32[]{:S(2)}) collective-permute-start(f32[5,64]{1,0:T(8,128)S(1)} %get-tuple-element.515), channel_id=1, source_target_pairs={{120,0},{0,8},{8,16},{16,24},{24,32},{32,40},{40,48},{48,56},{56,6... | collective-permute-start | bytes 3848 | tf_op jit(solution)/shard_map/while/body/eval_jaxpr/ppermute | solution.py:14
  301.3 9.3 %collective-permute-start.3 = (f32[5,64,128]{2,1,0:T(8,128)S(1)}, f32[5,64,128]{2,1,0:T(8,128)S(1)}, u32[]{:S(2)}, u32[]{:S(2)}) collective-permute-start(f32[5,64,128]{2,1,0:T(8,128)S(1)} %get-tuple-element.517), channel_id=1, source_target_pairs={{120,0},{0,8},{8,16},{16,24},{24,32},{32,40},{40,48},{48,56},{56,6... | collective-permute-start | bytes 491528 | tf_op jit(solution)/shard_map/while/body/eval_jaxpr/ppermute | solution.py:14
  301.4 9.2 %collective-permute-start.1 = (f32[5,64]{1,0:T(8,128)S(1)}, f32[5,64]{1,0:T(8,128)S(1)}, u32[]{:S(2)}, u32[]{:S(2)}) collective-permute-start(f32[5,64]{1,0:T(8,128)S(1)} %get-tuple-element.515), channel_id=1, source_target_pairs={{120,0},{0,8},{8,16},{16,24},{24,32},{32,40},{40,48},{48,56},{56,6... | collective-permute-start | bytes 3848 | tf_op jit(solution)/shard_map/while/body/eval_jaxpr/ppermute | solution.py:14
  348.8 9.3 %collective-permute-start.3 = (f32[5,64,128]{2,1,0:T(8,128)S(1)}, f32[5,64,128]{2,1,0:T(8,128)S(1)}, u32[]{:S(2)}, u32[]{:S(2)}) collective-permute-start(f32[5,64,128]{2,1,0:T(8,128)S(1)} %get-tuple-element.517), channel_id=1, source_target_pairs={{120,0},{0,8},{8,16},{16,24},{24,32},{32,40},{40,48},{48,56},{56,6... | collective-permute-start | bytes 491528 | tf_op jit(solution)/shard_map/while/body/eval_jaxpr/ppermute | solution.py:14
  396.3 9.3 %collective-permute-start.3 = (f32[5,64,128]{2,1,0:T(8,128)S(1)}, f32[5,64,128]{2,1,0:T(8,128)S(1)}, u32[]{:S(2)}, u32[]{:S(2)}) collective-permute-start(f32[5,64,128]{2,1,0:T(8,128)S(1)} %get-tuple-element.517), channel_id=1, source_target_pairs={{120,0},{0,8},{8,16},{16,24},{24,32},{32,40},{40,48},{48,56},{56,6... | collective-permute-start | bytes 491528 | tf_op jit(solution)/shard_map/while/body/eval_jaxpr/ppermute | solution.py:14
  443.8 9.3 %collective-permute-start.3 = (f32[5,64,128]{2,1,0:T(8,128)S(1)}, f32[5,64,128]{2,1,0:T(8,128)S(1)}, u32[]{:S(2)}, u32[]{:S(2)}) collective-permute-start(f32[5,64,128]{2,1,0:T(8,128)S(1)} %get-tuple-element.517), channel_id=1, source_target_pairs={{120,0},{0,8},{8,16},{16,24},{24,32},{32,40},{40,48},{48,56},{56,6... | collective-permute-start | bytes 491528 | tf_op jit(solution)/shard_map/while/body/eval_jaxpr/ppermute | solution.py:14
  443.9 9.2 %collective-permute-start.1 = (f32[5,64]{1,0:T(8,128)S(1)}, f32[5,64]{1,0:T(8,128)S(1)}, u32[]{:S(2)}, u32[]{:S(2)}) collective-permute-start(f32[5,64]{1,0:T(8,128)S(1)} %get-tuple-element.515), channel_id=1, source_target_pairs={{120,0},{0,8},{8,16},{16,24},{24,32},{32,40},{40,48},{48,56},{56,6... | collective-permute-start | bytes 3848 | tf_op jit(solution)/shard_map/while/body/eval_jaxpr/ppermute | solution.py:14
  491.3 9.3 %collective-permute-start.3 = (f32[5,64,128]{2,1,0:T(8,128)S(1)}, f32[5,64,128]{2,1,0:T(8,128)S(1)}, u32[]{:S(2)}, u32[]{:S(2)}) collective-permute-start(f32[5,64,128]{2,1,0:T(8,128)S(1)} %get-tuple-element.517), channel_id=1, source_target_pairs={{120,0},{0,8},{8,16},{16,24},{24,32},{32,40},{40,48},{48,56},{56,6... | collective-permute-start | bytes 491528 | tf_op jit(solution)/shard_map/while/body/eval_jaxpr/ppermute | solution.py:14
  491.4 9.2 %collective-permute-start.1 = (f32[5,64]{1,0:T(8,128)S(1)}, f32[5,64]{1,0:T(8,128)S(1)}, u32[]{:S(2)}, u32[]{:S(2)}) collective-permute-start(f32[5,64]{1,0:T(8,128)S(1)} %get-tuple-element.515), channel_id=1, source_target_pairs={{120,0},{0,8},{8,16},{16,24},{24,32},{32,40},{40,48},{48,56},{56,6... | collective-permute-start | bytes 3848 | tf_op jit(solution)/shard_map/while/body/eval_jaxpr/ppermute | solution.py:14
  538.8 9.3 %collective-permute-start.3 = (f32[5,64,128]{2,1,0:T(8,128)S(1)}, f32[5,64,128]{2,1,0:T(8,128)S(1)}, u32[]{:S(2)}, u32[]{:S(2)}) collective-permute-start(f32[5,64,128]{2,1,0:T(8,128)S(1)} %get-tuple-element.517), channel_id=1, source_target_pairs={{120,0},{0,8},{8,16},{16,24},{24,32},{32,40},{40,48},{48,56},{56,6... | collective-permute-start | bytes 491528 | tf_op jit(solution)/shard_map/while/body/eval_jaxpr/ppermute | solution.py:14
  538.9 9.2 %collective-permute-start.1 = (f32[5,64]{1,0:T(8,128)S(1)}, f32[5,64]{1,0:T(8,128)S(1)}, u32[]{:S(2)}, u32[]{:S(2)}) collective-permute-start(f32[5,64]{1,0:T(8,128)S(1)} %get-tuple-element.515), channel_id=1, source_target_pairs={{120,0},{0,8},{8,16},{16,24},{24,32},{32,40},{40,48},{48,56},{56,6... | collective-permute-start | bytes 3848 | tf_op jit(solution)/shard_map/while/body/eval_jaxpr/ppermute | solution.py:14
  586.3 9.3 %collective-permute-start.3 = (f32[5,64,128]{2,1,0:T(8,128)S(1)}, f32[5,64,128]{2,1,0:T(8,128)S(1)}, u32[]{:S(2)}, u32[]{:S(2)}) collective-permute-start(f32[5,64,128]{2,1,0:T(8,128)S(1)} %get-tuple-element.517), channel_id=1, source_target_pairs={{120,0},{0,8},{8,16},{16,24},{24,32},{32,40},{40,48},{48,56},{56,6... | collective-permute-start | bytes 491528 | tf_op jit(solution)/shard_map/while/body/eval_jaxpr/ppermute | solution.py:14
  633.9 9.3 %collective-permute-start.3 = (f32[5,64,128]{2,1,0:T(8,128)S(1)}, f32[5,64,128]{2,1,0:T(8,128)S(1)}, u32[]{:S(2)}, u32[]{:S(2)}) collective-permute-start(f32[5,64,128]{2,1,0:T(8,128)S(1)} %get-tuple-element.517), channel_id=1, source_target_pairs={{120,0},{0,8},{8,16},{16,24},{24,32},{32,40},{40,48},{48,56},{56,6... | collective-permute-start | bytes 491528 | tf_op jit(solution)/shard_map/while/body/eval_jaxpr/ppermute | solution.py:14
  681.4 9.3 %collective-permute-start.3 = (f32[5,64,128]{2,1,0:T(8,128)S(1)}, f32[5,64,128]{2,1,0:T(8,128)S(1)}, u32[]{:S(2)}, u32[]{:S(2)}) collective-permute-start(f32[5,64,128]{2,1,0:T(8,128)S(1)} %get-tuple-element.517), channel_id=1, source_target_pairs={{120,0},{0,8},{8,16},{16,24},{24,32},{32,40},{40,48},{48,56},{56,6... | collective-permute-start | bytes 491528 | tf_op jit(solution)/shard_map/while/body/eval_jaxpr/ppermute | solution.py:14
  728.9 9.3 %collective-permute-start.3 = (f32[5,64,128]{2,1,0:T(8,128)S(1)}, f32[5,64,128]{2,1,0:T(8,128)S(1)}, u32[]{:S(2)}, u32[]{:S(2)}) collective-permute-start(f32[5,64,128]{2,1,0:T(8,128)S(1)} %get-tuple-element.517), channel_id=1, source_target_pairs={{120,0},{0,8},{8,16},{16,24},{24,32},{32,40},{40,48},{48,56},{56,6... | collective-permute-start | bytes 491528 | tf_op jit(solution)/shard_map/while/body/eval_jaxpr/ppermute | solution.py:14
  (38 other events, 320.4 us)
Sparse Core Ops, SparseCore 0:
  789.3 40.7 reduce-scatter.1
where the time goes:
time: 850 us; the launch traced here: 837 us
  matrix products  434 us (51%)
  waiting for transfers between devices  181 us (21%)
  local copies, waits for them, and re-layouts  89.9 us (11%)
  loops' own time  78.7 us (9%)
  other arithmetic  32.1 us (4%)
  between operations  13.4 us (2%)
    dot_general x128, matrix products, block_step(): jnp.einsum('hrk,khd->hrd', probs, value_block, precision=lax.Precision.HI...  248 us
    dot_general x128, matrix products, block_step(): jnp.einsum('rhd,khd->hrk', query_heads, key_block, preferred_element_type...  181 us
    ppermute x61, waiting for transfers between devices, shifted(): return lax.ppermute(block, axis, route)  140 us
    another operation x16, loops' own time, attend(): lax.scan(block_step, carried, jnp.arange(block_count, dtype=jnp.int32))  77.3 us
    dynamic_slice x128, local copies, waits for them, and re-layouts, attend(): lax.scan(block_step, carried, jnp.arange(block_count, dtype=jnp.int32))  72.2 us
    reduce_scatter x1, waiting for transfers between devices, on_device(): lax.psum_scatter(partial_out, 'tensor', scatter_dimension=1, tiled=True)  41 us
    reduce_sum x128, other arithmetic, block_step(): totals = totals * factor + jnp.sum(probs, axis=2)  30.1 us
  transfers between devices with their start and end apart: 62, of which 32 were waited for; matrix products, arithmetic and copies ran while one was open for 0% of the time, Pallas kernels for 0%

commit v1 on v0

v1 whole, which is shorter than its diff:
```python
import math

import jax
import jax.numpy as jnp
from jax import lax
from jax.experimental import pallas as pl
from jax.experimental.pallas import tpu as pltpu
from jax.sharding import PartitionSpec as P

HD = 128
LOG2E = 1.4426950408889634
MESH = pl.DeviceIdType.MESH
NT = (((1,), (1,)), ((), ()))
NN = (((1,), (0,)), ((), ()))
F32, BF = jnp.float32, jnp.bfloat16

ROWS = 512
KEYS = 256


def on_device(queries, cached_keys, cached_values, out_weight):
    n_tm, n_te = lax.axis_size("tm"), lax.axis_size("tensor")
    own = queries.shape[0]
    rows = own * n_tm
    kv = cached_keys.shape[0]
    width = cached_keys.shape[1]
    heads = width // HD
    model = out_weight.shape[1]
    feat = model // n_te
    tile = min(ROWS, rows)
    tiles = rows // tile
    per_tile = tile // own
    scale = LOG2E / math.sqrt(HD)
    groups = [(0, 1), (1, 2), (2, heads)]

    def kernel(q_hbm, k_hbm, v_hbm, w_hbm, out, qbuf, kbuf, vbuf, wbuf, sbuf, mbuf, osend, orecv,
               att, psend, precv, q_sem, k_sem, v_sem, w_sem, qs, qr, os, orr, ps, pr):
        tm, te = lax.axis_index("tm"), lax.axis_index("tensor")

        def hcol(h):
            return pl.ds(pl.multiple_of(h * HD, HD), HD)

        def block(i):
            return pl.ds(pl.multiple_of(i * own, own), own)

        def k_load(h):
            return pltpu.make_async_copy(k_hbm.at[:, hcol(h)], kbuf.at[h], k_sem.at[h])

        def v_load(h):
            return pltpu.make_async_copy(v_hbm.at[:, hcol(h)], vbuf.at[h, :, pl.ds(0, HD)], v_sem.at[h])

        q_load = pltpu.make_async_copy(q_hbm, qbuf.at[block(tm), :], q_sem)
        w_load = pltpu.make_async_copy(w_hbm, wbuf, w_sem)
        q_load.start()
        k_load(0).start()
        v_load(0).start()

        barrier = pltpu.get_barrier_semaphore()

        def greet_tm(d, _):
            pl.semaphore_signal(barrier, inc=1, device_id={"tm": lax.rem(tm + d, n_tm)}, device_id_type=MESH)
            return 0

        def greet_te(d, _):
            pl.semaphore_signal(barrier, inc=1, device_id={"tensor": lax.rem(te + d, n_te)}, device_id_type=MESH)
            return 0

        lax.fori_loop(1, n_tm, greet_tm, 0)
        lax.fori_loop(1, n_te, greet_te, 0)

        def ones(h):
            def fill(i, _):
                vbuf[h, pl.ds(pl.multiple_of(i * 256, 256), 256), HD:] = jnp.ones((256, HD), BF)
                return 0
            lax.fori_loop(0, kv // 256, fill, 0)

        ones(0)
        pl.semaphore_wait(barrier, n_tm - 1 + n_te - 1)

        def q_copy(g, d):
            lo, hi = groups[g]
            cols = pl.ds(lo * HD, (hi - lo) * HD)
            return pltpu.make_async_remote_copy(
                src_ref=q_hbm.at[:, cols], dst_ref=qbuf.at[block(tm), cols],
                send_sem=qs.at[g, d], recv_sem=qr.at[g, d],
                device_id={"tm": lax.rem(tm + d, n_tm)}, device_id_type=MESH)

        def q_arrival(g, d):
            lo, hi = groups[g]
            cols = pl.ds(lo * HD, (hi - lo) * HD)
            return pltpu.make_async_remote_copy(
                src_ref=q_hbm.at[:, cols], dst_ref=qbuf.at[block(lax.rem(tm + n_tm - d, n_tm)), cols],
                send_sem=qs.at[g, d], recv_sem=qr.at[g, d],
                device_id={"tm": lax.rem(tm + d, n_tm)}, device_id_type=MESH)

        for g in range(len(groups)):
            def send_q(d, _, g=g):
                q_copy(g, d).start()
                return 0
            lax.fori_loop(1, n_tm, send_q, 0)

        for h in range(1, heads):
            k_load(h).start()
            v_load(h).start()
        w_load.start()
        for h in range(1, heads):
            ones(h)
        q_load.wait()

        def need_queries(g):
            def wait_q(d, _):
                q_arrival(g, d).wait_recv()
                return 0
            lax.fori_loop(1, n_tm, wait_q, 0)

        def step(t, do_s, do_p):
            h, r = t // tiles, lax.rem(t, tiles)
            hn, rn = (t + 1) // tiles, lax.rem(t + 1, tiles)
            cur, nxt = lax.rem(t, 2), lax.rem(t + 1, 2)
            mx = acc = None
            if do_s:
                qn = qbuf[pl.ds(pl.multiple_of(rn * tile, tile), tile), hcol(hn)]
            if do_p:
                m = mbuf[cur][:, :1]
            for c in range(kv // KEYS):
                ck = slice(c * KEYS, (c + 1) * KEYS)
                if do_s:
                    x = lax.dot_general(qn, kbuf[hn, ck, :], NT, preferred_element_type=F32)
                    sbuf[nxt, :, ck] = x
                    y = x[:, :HD]
                    for i in range(1, KEYS // HD):
                        y = jnp.maximum(y, x[:, i * HD:(i + 1) * HD])
                    mx = y if mx is None else jnp.maximum(mx, y)
                if do_p:
                    p = jnp.exp2(sbuf[cur, :, ck] * scale - m).astype(BF)
                    d = lax.dot_general(p, vbuf[h, ck, :], NN, preferred_element_type=F32)
                    acc = d if acc is None else acc + d
            if do_p:
                total = acc[:, HD:]
                lse = mbuf[cur] + jnp.log(total) * LOG2E
                hi = lse.astype(BF).astype(F32)
                mid = (lse - hi).astype(BF).astype(F32)
                low = lse - hi - mid
                lane = lax.broadcasted_iota(jnp.int32, (tile, HD), 1)
                stats = jnp.where(lane == 0, hi, jnp.where(lane == 1, mid, jnp.where(lane == 2, low, 0.0)))
                trow = pl.ds(pl.multiple_of(r * tile, tile), tile)
                osend[h, trow, :HD] = (acc[:, :HD] / total).astype(BF)
                osend[h, trow, HD:] = stats.astype(BF)
            if do_s:
                mbuf[nxt] = jnp.broadcast_to(jnp.max(mx, axis=1, keepdims=True) * scale, (tile, HD))

        def o_copy(h, d):
            to = lax.rem(tm + d, n_tm)
            return pltpu.make_async_remote_copy(
                src_ref=osend.at[h, block(to), :], dst_ref=orecv.at[h, tm],
                send_sem=os.at[h, d], recv_sem=orr.at[h, d],
                device_id={"tm": to}, device_id_type=MESH)

        def o_arrival(h, d):
            return pltpu.make_async_remote_copy(
                src_ref=osend.at[h, block(tm), :], dst_ref=orecv.at[h, lax.rem(tm + n_tm - d, n_tm)],
                send_sem=os.at[h, d], recv_sem=orr.at[h, d],
                device_id={"tm": lax.rem(tm + d, n_tm)}, device_id_type=MESH)

        def send_tile(t):
            h, r = t // tiles, lax.rem(t, tiles)

            def one(j, _):
                to = r * per_tile + lax.rem(tm + 1 + j, per_tile)
                d = lax.rem(to - tm + n_tm, n_tm)

                @pl.when(to != tm)
                def _():
                    o_copy(h, d).start()
                return 0
            lax.fori_loop(0, per_tile, one, 0)

        def combine(h):
            def wait_o(d, _):
                o_arrival(h, d).wait_recv()
                return 0
            lax.fori_loop(1, n_tm, wait_o, 0)
            orecv[h, tm] = osend[h, block(tm), :]
            stats = orecv[h, :, :, HD:].reshape(rows, HD)
            lse = lax.dot_general(stats, jnp.ones((HD, HD), BF), NN, preferred_element_type=F32).reshape(n_tm, own, HD)
            w = jnp.exp2(lse - jnp.max(lse, axis=0, keepdims=True))
            num = jnp.sum(w * orecv[h, :, :, :HD].astype(F32), axis=0)
            att[:, hcol(h)] = (num / jnp.sum(w, axis=0)).astype(BF)

        last = heads * tiles - 1
        need_queries(0)
        k_load(0).wait()
        step(-1 + 0 * tm, True, False)

        def body(t, _):
            for g in range(1, len(groups)):
                @pl.when(t + 1 == groups[g][0] * tiles)
                def _():
                    need_queries(g)
            h, r = t // tiles, lax.rem(t, tiles)

            @pl.when(r == tiles - 1)
            def _():
                k_load(h + 1).wait()

            @pl.when(r == 0)
            def _():
                v_load(h).wait()

            step(t, True, True)
            send_tile(t)

            @pl.when(jnp.logical_and(h >= 1, r == tiles - 1))
            def _():
                combine(h - 1)
            return 0

        lax.fori_loop(0, last, body, 0)
        if tiles == 1:
            v_load(heads - 1).wait()
        step(last + 0 * tm, False, True)
        send_tile(last)
        w_load.wait()
        combine(heads - 2)
        combine(heads - 1)

        def fcol(i):
            return pl.ds(pl.multiple_of(i * feat, feat), feat)

        def p_copy(d):
            return pltpu.make_async_remote_copy(
                src_ref=psend.at[d], dst_ref=precv.at[d],
                send_sem=ps.at[d], recv_sem=pr.at[d],
                device_id={"tensor": lax.rem(te + d, n_te)}, device_id_type=MESH)

        def project(d, _):
            part = lax.dot_general(att[...], wbuf[:, fcol(lax.rem(te + d, n_te))], NN, preferred_element_type=F32)
            psend[d] = part.astype(BF)
            p_copy(d).start()
            return 0

        lax.fori_loop(1, n_te, project, 0)
        out[...] = lax.dot_general(att[...], wbuf[:, fcol(te)], NN, preferred_element_type=F32)

        def gather_p(d, _):
            p_copy(d).wait_recv()
            out[...] += precv[d].astype(F32)
            return 0

        lax.fori_loop(1, n_te, gather_p, 0)

        def sent_p(d, _):
            p_copy(d).wait_send()
            return 0

        lax.fori_loop(1, n_te, sent_p, 0)

        def sent_tm(d, _):
            for g in range(len(groups)):
                q_copy(g, d).wait_send()
            for h in range(heads):
                o_copy(h, d).wait_send()
            return 0

        lax.fori_loop(1, n_tm, sent_tm, 0)

    any_ = pl.BlockSpec(memory_space=pl.ANY)
    dma = pltpu.SemaphoreType.DMA
    return pl.pallas_call(
        kernel,
        out_shape=jax.ShapeDtypeStruct((own, feat), F32),
        in_specs=[any_] * 4,
        out_specs=pl.BlockSpec(memory_space=pltpu.VMEM),
        scratch_shapes=[
            pltpu.VMEM((rows, width), BF),
            pltpu.VMEM((heads, kv, HD), BF),
            pltpu.VMEM((heads, kv, 2 * HD), BF),
            pltpu.VMEM((width, model), BF),
            pltpu.VMEM((2, tile, kv), F32),
            pltpu.VMEM((2, tile, HD), F32),
            pltpu.VMEM((heads, rows, 2 * HD), BF),
            pltpu.VMEM((heads, n_tm, own, 2 * HD), BF),
            pltpu.VMEM((own, width), BF),
            pltpu.VMEM((n_te, own, feat), BF),
            pltpu.VMEM((n_te, own, feat), BF),
            dma, dma((heads,)), dma((heads,)), dma,
            dma((len(groups), n_tm)), dma((len(groups), n_tm)),
            dma((heads, n_tm)), dma((heads, n_tm)),
            dma((n_te,)), dma((n_te,)),
        ],
        compiler_params=pltpu.CompilerParams(
            collective_id=0, has_side_effects=True, vmem_limit_bytes=60 * 2**20),
        name="late_uniting_attention",
    )(queries, cached_keys, cached_values, out_weight)


def solution(mesh):
    placed = (P("tm", "tensor"), P("tm", "tensor"), P("tm", "tensor"), P("tensor", None))
    return jax.shard_map(
        on_device, mesh=mesh, in_specs=placed, out_specs=P("tm", "tensor"), check_vma=False
    )
```

time: 850 us -> 77.6 us (0.09); the launches traced: 837 us -> 76.6 us
  matrix products: 434 us -> 0 us
  waiting for transfers between devices: 181 us -> 0 us
  local copies, waits for them, and re-layouts: 89.9 us -> 1.59 us
  loops' own time: 78.7 us -> 0 us
  Pallas kernels: 0 us -> 75 us
  other arithmetic: 32.1 us -> 0 us
  between operations: 13.4 us -> 0.01 us
    dot_general x257 -> x0, matrix products: 434 us -> none  [the longest x128 248 us: block_step(): jnp.einsum('hrk,khd->hrd', probs, value_block, precision=lax.Precision.HI...]
    ppermute x61 -> x0, waiting for transfers between devices: 140 us -> none  [shifted(): return lax.ppermute(block, axis, route)]
    another operation x17 -> x0, loops' own time: 78.7 us -> none  [the longest x16 77.3 us: attend(): lax.scan(block_step, carried, jnp.arange(block_count, dtype=jnp.int32))]
    pallas_call x0 -> x1, Pallas kernels: none -> 75 us  [on_device(): pl.pallas_call(kernel, out_shape=jax.ShapeDtypeStruct((own, feat), F32),...]
    dynamic_slice x128 -> x0, local copies, waits for them, and re-layouts: 72.2 us -> none  [attend(): lax.scan(block_step, carried, jnp.arange(block_count, dtype=jnp.int32))]
    reduce_scatter x1 -> x0, waiting for transfers between devices: 41 us -> none  [on_device(): lax.psum_scatter(partial_out, 'tensor', scatter_dimension=1, tiled=True)]
    reduce_sum x128 -> x0, other arithmetic: 30.1 us -> none  [block_step(): totals = totals * factor + jnp.sum(probs, axis=2)]
    unnamed x4 -> x1, local copies, waits for them, and re-layouts: 16.8 us -> 1.59 us
  transfers between devices with their start and end apart: 62 -> 0, of which waited for: 32 -> 0; matrix products, arithmetic and copies ran while one was open for 0% -> 0% of each run, Pallas kernels for 0% -> 0%
where the time goes in v1:
time: 77.6 us; the launch traced here: 76.6 us
  Pallas kernels  75 us (97%)
  local copies, waits for them, and re-layouts  1.59 us (2%)
    pallas_call x1, Pallas kernels, on_device(): pl.pallas_call(kernel, out_shape=jax.ShapeDtypeStruct((own, feat), F32),...  75 us
    unnamed x1, local copies, waits for them, and re-layouts  1.59 us

profile of v1, /device:TPU:0, one launch (start us, length us, event | category | flops | bytes accessed | tf_op | source)
XLA Modules:
  0.0 76.6 jit_solution(43039292594636602)
XLA Ops:
  0.0 75.0 %late_uniting_attention.1 = f32[64,640]{1,0:T(8,128)} custom-call(bf16[64,640]{1,0:T(8,128)(2,1)} %q_hbm.1, bf16[4096,640]{1,0:T(8,128)(2,1)} %k_hbm.1, bf16[4096,640]{1,0:T(8,128)(2,1)} %v_hbm.1, bf16[640,5120]{1,0:T(8,128)(2,1)} %w_hbm.1), custom_call_target="tpu_custom_call" | custom-call | tf_op jit(solution)/shard_map/late_uniting_attention/pallas_call | solution.py:269
  75.0 1.6 %copy.6 = f32[64,640]{1,0:T(8,128)} copy(f32[64,640]{1,0:T(8,128)} %late_uniting_attention.1) | data formatting | bytes 327680

commit v2 on v0

v2 whole, which is shorter than its diff:
```python
import math

import jax
import jax.numpy as jnp
from jax import lax
from jax.experimental import pallas as pl
from jax.experimental.pallas import tpu as pltpu
from jax.sharding import PartitionSpec as P

HD = 128
LOG2E = 1.4426950408889634
MESH = pl.DeviceIdType.MESH
NT = (((1,), (1,)), ((), ()))
NN = (((1,), (0,)), ((), ()))
F32, BF = jnp.float32, jnp.bfloat16

KEYS = 256
TILES = 2


def on_device(queries, cached_keys, cached_values, out_weight):
    n_tm, n_te = lax.axis_size("tm"), lax.axis_size("tensor")
    chips = n_tm // 2
    own = queries.shape[0]
    kv = cached_keys.shape[0]
    width = cached_keys.shape[1]
    heads = width // HD
    model = out_weight.shape[1]
    feat = model // n_te
    part = own // TILES
    half = part * chips
    tile = 2 * half
    steps = TILES * heads
    scale = LOG2E / math.sqrt(HD)
    groups = [(0, 0, 2), (0, 2, heads)] + [(r, 0, heads) for r in range(1, TILES)]

    def kernel(q_hbm, k_hbm, v_hbm, w_hbm, out, qbuf, kbuf, vbuf, wbuf, s_a, s_b, m_a, m_b, keep, give, taken,
               osend, orecv, att, psend, precv,
               q_sem, k_sem, v_sem, w_sem, qs, qr, fs, fr, gs, gr, os, orr, ps, pr):
        tm, te = lax.axis_index("tm"), lax.axis_index("tensor")
        core, chip = lax.rem(tm, 2), tm // 2
        sibling = tm + 1 - 2 * core

        def hcol(h):
            return pl.ds(pl.multiple_of(h * HD, HD), HD)

        def fcol(i):
            return pl.ds(pl.multiple_of(i * feat, feat), feat)

        def to_chip(d):
            return {"tm": 2 * lax.rem(chip + d, chips) + core}

        def to_group(d):
            return {"tensor": lax.rem(te + d, n_te)}

        def block(d):
            return pl.ds(pl.multiple_of(lax.rem(chip + chips - d, chips) * part, part), part)

        def each(lo, hi, f):
            def go(i, _):
                f(i)
                return 0
            lax.fori_loop(lo, hi, go, 0)

        def k_load(h):
            return pltpu.make_async_copy(k_hbm.at[:, hcol(h)], kbuf.at[h], k_sem.at[h])

        def v_load(h):
            return pltpu.make_async_copy(v_hbm.at[:, hcol(h)], vbuf.at[h, :, pl.ds(0, HD)], v_sem.at[h])

        def q_load(r):
            return pltpu.make_async_copy(q_hbm.at[pl.ds(r * part, part), :], qbuf.at[r, block(0), :], q_sem.at[r])

        w_load = pltpu.make_async_copy(w_hbm, wbuf, w_sem)
        for r in range(TILES):
            q_load(r).start()
        for h in range(heads):
            k_load(h).start()
            v_load(h).start()
        w_load.start()

        barrier = pltpu.get_barrier_semaphore()
        pl.semaphore_signal(barrier, inc=1, device_id={"tm": sibling}, device_id_type=MESH)
        each(1, chips, lambda d: pl.semaphore_signal(barrier, inc=1, device_id=to_chip(d), device_id_type=MESH))
        each(1, n_te, lambda d: pl.semaphore_signal(barrier, inc=1, device_id=to_group(d), device_id_type=MESH))

        def fill(i):
            for h in range(heads):
                vbuf[h, pl.ds(pl.multiple_of(i * 256, 256), 256), HD:] = jnp.ones((256, HD), BF)

        each(0, kv // 256, fill)
        for r in range(TILES):
            q_load(r).wait()
        pl.semaphore_wait(barrier, 1 + chips - 1 + n_te - 1)

        def q_copy(g, d, at):
            r, lo, hi = groups[g]
            cols = pl.ds(lo * HD, (hi - lo) * HD)
            return pltpu.make_async_remote_copy(
                src_ref=q_hbm.at[pl.ds(r * part, part), cols], dst_ref=qbuf.at[r, block(at), cols],
                send_sem=qs.at[g, d], recv_sem=qr.at[g, d], device_id=to_chip(d), device_id_type=MESH)

        def q_pass(g):
            r, lo, hi = groups[g]
            cols = pl.ds(lo * HD, (hi - lo) * HD)
            return pltpu.make_async_remote_copy(
                src_ref=qbuf.at[r, pl.ds(0, half), cols], dst_ref=qbuf.at[r, pl.ds(half, half), cols],
                send_sem=fs.at[g], recv_sem=fr.at[g], device_id={"tm": sibling}, device_id_type=MESH)

        def q_send(g):
            each(1, chips, lambda d: q_copy(g, d, 0).start())

        def q_relay(g):
            each(1, chips, lambda d: q_copy(g, d, d).wait_recv())
            q_pass(g).start()

        def step(t, cur, nxt, mcur, mnxt):
            h = lax.rem(t, heads)
            hn, rn = lax.rem(t + 1, heads), (t + 1) // heads
            mx = acc = None
            if nxt is not None:
                qn = qbuf[rn, :, hcol(hn)]
            if cur is not None:
                m = mcur[:, :1]
            for c in range(kv // KEYS):
                ck = slice(c * KEYS, (c + 1) * KEYS)
                if nxt is not None:
                    x = lax.dot_general(qn, kbuf[hn, ck, :], NT, preferred_element_type=F32)
                    nxt[:, ck] = x
                    y = x[:, :HD]
                    for i in range(1, KEYS // HD):
                        y = jnp.maximum(y, x[:, i * HD:(i + 1) * HD])
                    mx = y if mx is None else jnp.maximum(mx, y)
                if cur is not None:
                    p = jnp.exp2(cur[:, ck] * scale - m).astype(BF)
                    d = lax.dot_general(p, vbuf[h, ck, :], NN, preferred_element_type=F32)
                    acc = d if acc is None else acc + d
            if cur is not None:
                total = acc[:, HD:]
                lse = mcur[...] + jnp.log(total) * LOG2E
                mean = acc[:, :HD] / total
                keep[t, :, :HD] = mean[:half]
                keep[t, :, HD:] = lse[:half]
                give[t, :, :HD] = mean[half:]
                give[t, :, HD:] = lse[half:]
                to_sibling(t).start()
            if nxt is not None:
                mnxt[...] = jnp.broadcast_to(jnp.max(mx, axis=1, keepdims=True) * scale, (tile, HD))

        def to_sibling(t):
            return pltpu.make_async_remote_copy(
                src_ref=give.at[t], dst_ref=taken.at[t], send_sem=gs.at[t], recv_sem=gr.at[t],
                device_id={"tm": sibling}, device_id_type=MESH)

        def o_copy(t, d, at):
            return pltpu.make_async_remote_copy(
                src_ref=osend.at[t, lax.rem(chip + d, chips)], dst_ref=orecv.at[t, lax.rem(chip + chips - at, chips)],
                send_sem=os.at[t, d], recv_sem=orr.at[t, d], device_id=to_chip(d), device_id_type=MESH)

        def merge(t):
            to_sibling(t).wait_recv()
            la, lb = keep[t, :, HD:], taken[t, :, HD:]
            top = jnp.maximum(la, lb)
            wa, wb = jnp.exp2(la - top), jnp.exp2(lb - top)
            total = wa + wb
            mean = (wa * keep[t, :, :HD] + wb * taken[t, :, :HD]) / total
            lse = top + jnp.log(total) * LOG2E
            hi = lse.astype(BF).astype(F32)
            mid = (lse - hi).astype(BF).astype(F32)
            low = lse - hi - mid
            lane = lax.broadcasted_iota(jnp.int32, (half, HD), 1)
            stats = jnp.where(lane == 0, hi, jnp.where(lane == 1, mid, jnp.where(lane == 2, low, 0.0)))
            osend[t, :, :, :HD] = mean.astype(BF).reshape(chips, part, HD)
            osend[t, :, :, HD:] = stats.astype(BF).reshape(chips, part, HD)
            each(1, chips, lambda d: o_copy(t, d, 0).start())
            orecv[t, chip] = osend[t, chip]

        def combine(t):
            each(1, chips, lambda d: o_copy(t, d, d).wait_recv())
            stats = orecv[t, :, :, HD:].reshape(half, HD)
            lse = lax.dot_general(stats, jnp.ones((HD, HD), BF), NN, preferred_element_type=F32)
            lse = lse.reshape(chips, part, HD)
            w = jnp.exp2(lse - jnp.max(lse, axis=0, keepdims=True))
            num = jnp.sum(w * orecv[t, :, :, :HD].astype(F32), axis=0)
            att[t // heads, :, hcol(lax.rem(t, heads))] = (num / jnp.sum(w, axis=0)).astype(BF)

        def p_copy(r, d):
            return pltpu.make_async_remote_copy(
                src_ref=psend.at[r, d], dst_ref=precv.at[r, d], send_sem=ps.at[r, d], recv_sem=pr.at[r, d],
                device_id=to_group(d), device_id_type=MESH)

        def project(r):
            def share(d):
                product = lax.dot_general(
                    att[r], wbuf[:, fcol(lax.rem(te + d, n_te))], NN, preferred_element_type=F32)
                psend[r, d] = product.astype(BF)
                p_copy(r, d).start()
            each(1, n_te, share)
            out[r * part:(r + 1) * part, :] = lax.dot_general(
                att[r], wbuf[:, fcol(te)], NN, preferred_element_type=F32)

        def unite(r):
            def add(d):
                p_copy(r, d).wait_recv()
                out[r * part:(r + 1) * part, :] += precv[r, d].astype(F32)
            each(1, n_te, add)

        def before(t):
            h, hn = lax.rem(t, heads), lax.rem(t + 1, heads)
            for g in range(1, len(groups)):
                r, lo, _ = groups[g]

                @pl.when(t + 1 == r * heads + lo)
                def _(g=g):
                    q_pass(g).wait_recv()

            @pl.when(t + 1 < heads)
            def _():
                k_load(hn).wait()

            @pl.when(t < heads)
            def _():
                v_load(h).wait()

        def after(t):
            for g in range(1, len(groups)):
                @pl.when(t == g - 1)
                def _(g=g):
                    q_relay(g)

            @pl.when(t >= 1)
            def _():
                merge(t - 1)

            @pl.when(t >= 2)
            def _():
                combine(t - 2)

            for r in range(TILES - 1):
                @pl.when(t == (r + 1) * heads + 1)
                def _(r=r):
                    if r == 0:
                        w_load.wait()
                    project(r)

        q_send(0)
        q_relay(0)
        for g in range(1, len(groups)):
            q_send(g)
        k_load(0).wait()
        q_pass(0).wait_recv()
        step(0 * tm - 1, None, s_a, None, m_a)

        def pair(u, _):
            before(2 * u)
            step(2 * u, s_a, s_b, m_a, m_b)
            after(2 * u)
            before(2 * u + 1)
            step(2 * u + 1, s_b, s_a, m_b, m_a)
            after(2 * u + 1)
            return 0

        last = 0 * tm + steps - 1
        lax.fori_loop(0, (steps - 1) // 2, pair, 0)
        if steps % 2 == 0:
            before(last - 1)
            step(last - 1, s_a, s_b, m_a, m_b)
            after(last - 1)
        end = (s_b, m_b) if steps % 2 == 0 else (s_a, m_a)
        before(last)
        step(last, end[0], None, end[1], None)
        after(last)
        merge(last)
        combine(last - 1)
        combine(last)
        if TILES == 1:
            w_load.wait()
        project(TILES - 1)
        for r in range(TILES):
            unite(r)

        def sent(d):
            for g in range(len(groups)):
                q_copy(g, d, 0).wait_send()
            each(0, steps, lambda t: o_copy(t, d, 0).wait_send())

        each(1, chips, sent)
        for g in range(len(groups)):
            q_pass(g).wait_send()
        each(0, steps, lambda t: to_sibling(t).wait_send())
        for r in range(TILES):
            each(1, n_te, lambda d: p_copy(r, d).wait_send())

    any_ = pl.BlockSpec(memory_space=pl.ANY)
    dma = pltpu.SemaphoreType.DMA
    n_g = len(groups)
    return pl.pallas_call(
        kernel,
        out_shape=jax.ShapeDtypeStruct((own, feat), F32),
        in_specs=[any_] * 4,
        out_specs=pl.BlockSpec(memory_space=pltpu.VMEM),
        scratch_shapes=[
            pltpu.VMEM((TILES, tile, width), BF),
            pltpu.VMEM((heads, kv, HD), BF),
            pltpu.VMEM((heads, kv, 2 * HD), BF),
            pltpu.VMEM((width, model), BF),
            pltpu.VMEM((tile, kv), F32),
            pltpu.VMEM((tile, kv), F32),
            pltpu.VMEM((tile, HD), F32),
            pltpu.VMEM((tile, HD), F32),
            pltpu.VMEM((steps, half, 2 * HD), F32),
            pltpu.VMEM((steps, half, 2 * HD), F32),
            pltpu.VMEM((steps, half, 2 * HD), F32),
            pltpu.VMEM((steps, chips, part, 2 * HD), BF),
            pltpu.VMEM((steps, chips, part, 2 * HD), BF),
            pltpu.VMEM((TILES, part, width), BF),
            pltpu.VMEM((TILES, n_te, part, feat), BF),
            pltpu.VMEM((TILES, n_te, part, feat), BF),
            dma((TILES,)), dma((heads,)), dma((heads,)), dma,
            dma((n_g, chips)), dma((n_g, chips)), dma((n_g,)), dma((n_g,)),
            dma((steps,)), dma((steps,)),
            dma((steps, chips)), dma((steps, chips)),
            dma((TILES, n_te)), dma((TILES, n_te)),
        ],
        compiler_params=pltpu.CompilerParams(
            collective_id=0, has_side_effects=True, vmem_limit_bytes=60 * 2**20),
        name="late_uniting_attention",
    )(queries, cached_keys, cached_values, out_weight)


def solution(mesh):
    placed = (P("tm", "tensor"), P("tm", "tensor"), P("tm", "tensor"), P("tensor", None))
    return jax.shard_map(
        on_device, mesh=mesh, in_specs=placed, out_specs=P("tm", "tensor"), check_vma=False
    )
```

time: 850 us -> 74.9 us (0.09); the launches traced: 837 us -> 74.7 us
  matrix products: 434 us -> 0 us
  waiting for transfers between devices: 181 us -> 0 us
  local copies, waits for them, and re-layouts: 89.9 us -> 1.59 us
  loops' own time: 78.7 us -> 0 us
  Pallas kernels: 0 us -> 73.1 us
  other arithmetic: 32.1 us -> 0 us
  between operations: 13.4 us -> 0.01 us
    dot_general x257 -> x0, matrix products: 434 us -> none  [the longest x128 248 us: block_step(): jnp.einsum('hrk,khd->hrd', probs, value_block, precision=lax.Precision.HI...]
    ppermute x61 -> x0, waiting for transfers between devices: 140 us -> none  [shifted(): return lax.ppermute(block, axis, route)]
    another operation x17 -> x0, loops' own time: 78.7 us -> none  [the longest x16 77.3 us: attend(): lax.scan(block_step, carried, jnp.arange(block_count, dtype=jnp.int32))]
    pallas_call x0 -> x1, Pallas kernels: none -> 73.1 us  [on_device(): pl.pallas_call(kernel, out_shape=jax.ShapeDtypeStruct((own, feat), F32),...]
    dynamic_slice x128 -> x0, local copies, waits for them, and re-layouts: 72.2 us -> none  [attend(): lax.scan(block_step, carried, jnp.arange(block_count, dtype=jnp.int32))]
    reduce_scatter x1 -> x0, waiting for transfers between devices: 41 us -> none  [on_device(): lax.psum_scatter(partial_out, 'tensor', scatter_dimension=1, tiled=True)]
    reduce_sum x128 -> x0, other arithmetic: 30.1 us -> none  [block_step(): totals = totals * factor + jnp.sum(probs, axis=2)]
    unnamed x4 -> x1, local copies, waits for them, and re-layouts: 16.8 us -> 1.59 us
  transfers between devices with their start and end apart: 62 -> 0, of which waited for: 32 -> 0; matrix products, arithmetic and copies ran while one was open for 0% -> 0% of each run, Pallas kernels for 0% -> 0%
where the time goes in v2:
time: 74.9 us; the launch traced here: 74.7 us
  Pallas kernels  73.1 us (98%)
  local copies, waits for them, and re-layouts  1.59 us (2%)
    pallas_call x1, Pallas kernels, on_device(): pl.pallas_call(kernel, out_shape=jax.ShapeDtypeStruct((own, feat), F32),...  73.1 us
    unnamed x1, local copies, waits for them, and re-layouts  1.59 us

profile of v2, /device:TPU:0, one launch (start us, length us, event | category | flops | bytes accessed | tf_op | source)
XLA Modules:
  0.0 74.7 jit_solution(653863669382624466)
XLA Ops:
  0.0 73.1 %late_uniting_attention.1 = f32[64,640]{1,0:T(8,128)} custom-call(bf16[64,640]{1,0:T(8,128)(2,1)} %q_hbm.1, bf16[4096,640]{1,0:T(8,128)(2,1)} %k_hbm.1, bf16[4096,640]{1,0:T(8,128)(2,1)} %v_hbm.1, bf16[640,5120]{1,0:T(8,128)(2,1)} %w_hbm.1), custom_call_target="tpu_custom_call" | custom-call | tf_op jit(solution)/shard_map/late_uniting_attention/pallas_call | solution.py:297
  73.2 1.6 %copy.6 = f32[64,640]{1,0:T(8,128)} copy(f32[64,640]{1,0:T(8,128)} %late_uniting_attention.1) | data formatting | bytes 327680

commit v3 on v2

--- a/solution.py
+++ b/solution.py
@@ -16,6 +16,7 @@
 
 KEYS = 256
 TILES = 2
+LAG = 3
 
 
 def on_device(queries, cached_keys, cached_values, out_weight):
@@ -32,11 +33,12 @@
     tile = 2 * half
     steps = TILES * heads
     scale = LOG2E / math.sqrt(HD)
-    groups = [(0, 0, 2), (0, 2, heads)] + [(r, 0, heads) for r in range(1, TILES)]
+    groups = [(0, 0, 1), (0, 1, 2), (0, 2, heads)] + [(r, 0, heads) for r in range(1, TILES)]
+    direct = 3
 
     def kernel(q_hbm, k_hbm, v_hbm, w_hbm, out, qbuf, kbuf, vbuf, wbuf, s_a, s_b, m_a, m_b, keep, give, taken,
-               osend, orecv, att, psend, precv,
-               q_sem, k_sem, v_sem, w_sem, qs, qr, fs, fr, gs, gr, os, orr, ps, pr):
+               osend, orecv, att, shares, psend, precv,
+               q_sem, k_sem, v_sem, w_sem, qs, qr, xs, xr, fs, fr, gs, gr, os, orr, ps, pr):
         tm, te = lax.axis_index("tm"), lax.axis_index("tensor")
         core, chip = lax.rem(tm, 2), tm // 2
         sibling = tm + 1 - 2 * core
@@ -82,6 +84,8 @@
         barrier = pltpu.get_barrier_semaphore()
         pl.semaphore_signal(barrier, inc=1, device_id={"tm": sibling}, device_id_type=MESH)
         each(1, chips, lambda d: pl.semaphore_signal(barrier, inc=1, device_id=to_chip(d), device_id_type=MESH))
+        each(1, chips, lambda d: pl.semaphore_signal(
+            barrier, inc=1, device_id={"tm": 2 * lax.rem(chip + d, chips) + 1 - core}, device_id_type=MESH))
         each(1, n_te, lambda d: pl.semaphore_signal(barrier, inc=1, device_id=to_group(d), device_id_type=MESH))
 
         def fill(i):
@@ -91,7 +95,7 @@
         each(0, kv // 256, fill)
         for r in range(TILES):
             q_load(r).wait()
-        pl.semaphore_wait(barrier, 1 + chips - 1 + n_te - 1)
+        pl.semaphore_wait(barrier, n_tm - 1 + n_te - 1)
 
         def q_copy(g, d, at):
             r, lo, hi = groups[g]
@@ -100,6 +104,15 @@
                 src_ref=q_hbm.at[pl.ds(r * part, part), cols], dst_ref=qbuf.at[r, block(at), cols],
                 send_sem=qs.at[g, d], recv_sem=qr.at[g, d], device_id=to_chip(d), device_id_type=MESH)
 
+        def q_cross(g, d, at):
+            r, lo, hi = groups[g]
+            cols = pl.ds(lo * HD, (hi - lo) * HD)
+            place = pl.ds(pl.multiple_of(half + lax.rem(chip + chips - at, chips) * part, part), part)
+            return pltpu.make_async_remote_copy(
+                src_ref=q_hbm.at[pl.ds(r * part, part), cols], dst_ref=qbuf.at[r, place, cols],
+                send_sem=xs.at[g, d], recv_sem=xr.at[g, d],
+                device_id={"tm": 2 * lax.rem(chip + d, chips) + 1 - core}, device_id_type=MESH)
+
         def q_pass(g):
             r, lo, hi = groups[g]
             cols = pl.ds(lo * HD, (hi - lo) * HD)
@@ -108,7 +121,21 @@
                 send_sem=fs.at[g], recv_sem=fr.at[g], device_id={"tm": sibling}, device_id_type=MESH)
 
         def q_send(g):
-            each(1, chips, lambda d: q_copy(g, d, 0).start())
+            if g < direct:
+                q_cross(g, 0, 0).start()
+
+            def one(d):
+                q_copy(g, d, 0).start()
+                if g < direct:
+                    q_cross(g, d, 0).start()
+            each(1, chips, one)
+
+        def q_need(g):
+            if g < direct:
+                each(1, chips, lambda d: q_copy(g, d, d).wait_recv())
+                each(0, chips, lambda d: q_cross(g, d, d).wait_recv())
+            else:
+                q_pass(g).wait_recv()
 
         def q_relay(g):
             each(1, chips, lambda d: q_copy(g, d, d).wait_recv())
@@ -189,15 +216,24 @@
                 src_ref=psend.at[r, d], dst_ref=precv.at[r, d], send_sem=ps.at[r, d], recv_sem=pr.at[r, d],
                 device_id=to_group(d), device_id_type=MESH)
 
+        most = width - HD
+
+        def prepare(r):
+            def share(d):
+                shares[d] = lax.dot_general(
+                    att[r, :, :most], wbuf[:most, fcol(lax.rem(te + d, n_te))], NN, preferred_element_type=F32)
+            each(0, n_te, share)
+
         def project(r):
+            def product(d):
+                return shares[d] + lax.dot_general(
+                    att[r, :, most:], wbuf[most:, fcol(lax.rem(te + d, n_te))], NN, preferred_element_type=F32)
+
             def share(d):
-                product = lax.dot_general(
-                    att[r], wbuf[:, fcol(lax.rem(te + d, n_te))], NN, preferred_element_type=F32)
-                psend[r, d] = product.astype(BF)
+                psend[r, d] = product(d).astype(BF)
                 p_copy(r, d).start()
             each(1, n_te, share)
-            out[r * part:(r + 1) * part, :] = lax.dot_general(
-                att[r], wbuf[:, fcol(te)], NN, preferred_element_type=F32)
+            out[r * part:(r + 1) * part, :] = product(0)
 
         def unite(r):
             def add(d):
@@ -212,7 +248,7 @@
 
                 @pl.when(t + 1 == r * heads + lo)
                 def _(g=g):
-                    q_pass(g).wait_recv()
+                    q_need(g)
 
             @pl.when(t + 1 < heads)
             def _():
@@ -223,8 +259,8 @@
                 v_load(h).wait()
 
         def after(t):
-            for g in range(1, len(groups)):
-                @pl.when(t == g - 1)
+            for g in range(direct, len(groups)):
+                @pl.when(t == (groups[g][0] - 1) * heads + 1)
                 def _(g=g):
                     q_relay(g)
 
@@ -232,23 +268,24 @@
             def _():
                 merge(t - 1)
 
-            @pl.when(t >= 2)
+            @pl.when(t >= LAG)
             def _():
-                combine(t - 2)
+                combine(t - LAG)
 
             for r in range(TILES - 1):
-                @pl.when(t == (r + 1) * heads + 1)
+                @pl.when(t == (r + 1) * heads - 1 + LAG)
                 def _(r=r):
                     if r == 0:
                         w_load.wait()
+                    prepare(r)
                     project(r)
 
         q_send(0)
-        q_relay(0)
-        for g in range(1, len(groups)):
+        q_send(1)
+        k_load(0).wait()
+        q_need(0)
+        for g in range(2, len(groups)):
             q_send(g)
-        k_load(0).wait()
-        q_pass(0).wait_recv()
         step(0 * tm - 1, None, s_a, None, m_a)
 
         def pair(u, _):
@@ -271,10 +308,10 @@
         step(last, end[0], None, end[1], None)
         after(last)
         merge(last)
-        combine(last - 1)
+        for i in range(LAG - 1, 0, -1):
+            combine(last - i)
+        prepare(TILES - 1)
         combine(last)
-        if TILES == 1:
-            w_load.wait()
         project(TILES - 1)
         for r in range(TILES):
             unite(r)
@@ -282,11 +319,16 @@
         def sent(d):
             for g in range(len(groups)):
                 q_copy(g, d, 0).wait_send()
+                if g < direct:
+                    q_cross(g, d, 0).wait_send()
             each(0, steps, lambda t: o_copy(t, d, 0).wait_send())
 
         each(1, chips, sent)
         for g in range(len(groups)):
-            q_pass(g).wait_send()
+            if g < direct:
+                q_cross(g, 0, 0).wait_send()
+            else:
+                q_pass(g).wait_send()
         each(0, steps, lambda t: to_sibling(t).wait_send())
         for r in range(TILES):
             each(1, n_te, lambda d: p_copy(r, d).wait_send())
@@ -314,10 +356,11 @@
             pltpu.VMEM((steps, chips, part, 2 * HD), BF),
             pltpu.VMEM((steps, chips, part, 2 * HD), BF),
             pltpu.VMEM((TILES, part, width), BF),
+            pltpu.VMEM((n_te, part, feat), F32),
             pltpu.VMEM((TILES, n_te, part, feat), BF),
             pltpu.VMEM((TILES, n_te, part, feat), BF),
             dma((TILES,)), dma((heads,)), dma((heads,)), dma,
-            dma((n_g, chips)), dma((n_g, chips)), dma((n_g,)), dma((n_g,)),
+            dma((n_g, chips)), dma((n_g, chips)), dma((n_g, chips)), dma((n_g, chips)), dma((n_g,)), dma((n_g,)),
             dma((steps,)), dma((steps,)),
             dma((steps, chips)), dma((steps, chips)),
             dma((TILES, n_te)), dma((TILES, n_te)),

time: 74.9 us -> 71.4 us (0.953)
  Pallas kernels: 73.1 us -> 69.7 us
    pallas_call x1, Pallas kernels: 73.1 us -> 69.7 us  [on_device(): pl.pallas_call(kernel, out_shape=jax.ShapeDtypeStruct((own, feat), F32),...]
where the time goes in v3:
time: 71.4 us; the launch traced here: 71.3 us
  Pallas kernels  69.7 us (98%)
  local copies, waits for them, and re-layouts  1.59 us (2%)
    pallas_call x1, Pallas kernels, on_device(): pl.pallas_call(kernel, out_shape=jax.ShapeDtypeStruct((own, feat), F32),...  69.7 us
    unnamed x1, local copies, waits for them, and re-layouts  1.59 us

profile of v3, /device:TPU:0, one launch (start us, length us, event | category | flops | bytes accessed | tf_op | source)
XLA Modules:
  0.0 71.3 jit_solution(13592972201683986335)
XLA Ops:
  0.0 69.7 %late_uniting_attention.1 = f32[64,640]{1,0:T(8,128)} custom-call(bf16[64,640]{1,0:T(8,128)(2,1)} %q_hbm.1, bf16[4096,640]{1,0:T(8,128)(2,1)} %k_hbm.1, bf16[4096,640]{1,0:T(8,128)(2,1)} %v_hbm.1, bf16[640,5120]{1,0:T(8,128)(2,1)} %w_hbm.1), custom_call_target="tpu_custom_call" | custom-call | tf_op jit(solution)/shard_map/late_uniting_attention/pallas_call | solution.py:339
  69.7 1.6 %copy.6 = f32[64,640]{1,0:T(8,128)} copy(f32[64,640]{1,0:T(8,128)} %late_uniting_attention.1) | data formatting | bytes 327680

commit v4 on v3

--- a/solution.py
+++ b/solution.py
@@ -33,8 +33,8 @@
     tile = 2 * half
     steps = TILES * heads
     scale = LOG2E / math.sqrt(HD)
-    groups = [(0, 0, 1), (0, 1, 2), (0, 2, heads)] + [(r, 0, heads) for r in range(1, TILES)]
-    direct = 3
+    groups = [(0, h, h + 1) for h in range(heads)] + [(r, 0, heads) for r in range(1, TILES)]
+    direct = heads
 
     def kernel(q_hbm, k_hbm, v_hbm, w_hbm, out, qbuf, kbuf, vbuf, wbuf, s_a, s_b, m_a, m_b, keep, give, taken,
                osend, orecv, att, shares, psend, precv,
@@ -144,35 +144,32 @@
         def step(t, cur, nxt, mcur, mnxt):
             h = lax.rem(t, heads)
             hn, rn = lax.rem(t + 1, heads), (t + 1) // heads
-            mx = acc = None
-            if nxt is not None:
-                qn = qbuf[rn, :, hcol(hn)]
-            if cur is not None:
-                m = mcur[:, :1]
+            mx, acc = [None, None], [None, None]
+            parts = [slice(0, half), slice(half, tile)]
             for c in range(kv // KEYS):
                 ck = slice(c * KEYS, (c + 1) * KEYS)
-                if nxt is not None:
-                    x = lax.dot_general(qn, kbuf[hn, ck, :], NT, preferred_element_type=F32)
-                    nxt[:, ck] = x
-                    y = x[:, :HD]
-                    for i in range(1, KEYS // HD):
-                        y = jnp.maximum(y, x[:, i * HD:(i + 1) * HD])
-                    mx = y if mx is None else jnp.maximum(mx, y)
-                if cur is not None:
-                    p = jnp.exp2(cur[:, ck] * scale - m).astype(BF)
-                    d = lax.dot_general(p, vbuf[h, ck, :], NN, preferred_element_type=F32)
-                    acc = d if acc is None else acc + d
+                for i, rs in enumerate(parts):
+                    if nxt is not None:
+                        qn = qbuf[rn, rs, hcol(hn)]
+                        x = lax.dot_general(qn, kbuf[hn, ck, :], NT, preferred_element_type=F32)
+                        nxt[rs, ck] = x
+                        y = x[:, :HD]
+                        for n in range(1, KEYS // HD):
+                            y = jnp.maximum(y, x[:, n * HD:(n + 1) * HD])
+                        mx[i] = y if c == 0 else jnp.maximum(mx[i], y)
+                    if cur is not None:
+                        p = jnp.exp2(cur[rs, ck] * scale - mcur[rs, :1]).astype(BF)
+                        d = lax.dot_general(p, vbuf[h, ck, :], NN, preferred_element_type=F32)
+                        acc[i] = d if c == 0 else acc[i] + d
             if cur is not None:
-                total = acc[:, HD:]
-                lse = mcur[...] + jnp.log(total) * LOG2E
-                mean = acc[:, :HD] / total
-                keep[t, :, :HD] = mean[:half]
-                keep[t, :, HD:] = lse[:half]
-                give[t, :, :HD] = mean[half:]
-                give[t, :, HD:] = lse[half:]
+                for i, put in ((1, give), (0, keep)):
+                    total = acc[i][:, HD:]
+                    put[t, :, :HD] = acc[i][:, :HD] / total
+                    put[t, :, HD:] = mcur[parts[i], :] + jnp.log(total) * LOG2E
                 to_sibling(t).start()
             if nxt is not None:
-                mnxt[...] = jnp.broadcast_to(jnp.max(mx, axis=1, keepdims=True) * scale, (tile, HD))
+                for i, rs in enumerate(parts):
+                    mnxt[rs, :] = jnp.broadcast_to(jnp.max(mx[i], axis=1, keepdims=True) * scale, (half, HD))
 
         def to_sibling(t):
             return pltpu.make_async_remote_copy(
@@ -280,12 +277,10 @@
                     prepare(r)
                     project(r)
 
-        q_send(0)
-        q_send(1)
+        for g in range(len(groups)):
+            q_send(g)
         k_load(0).wait()
         q_need(0)
-        for g in range(2, len(groups)):
-            q_send(g)
         step(0 * tm - 1, None, s_a, None, m_a)
 
         def pair(u, _):
@@ -311,10 +306,10 @@
         for i in range(LAG - 1, 0, -1):
             combine(last - i)
         prepare(TILES - 1)
+        for r in range(TILES - 1):
+            unite(r)
         combine(last)
         project(TILES - 1)
-        for r in range(TILES):
-            unite(r)
 
         def sent(d):
             for g in range(len(groups)):
@@ -330,6 +325,7 @@
             else:
                 q_pass(g).wait_send()
         each(0, steps, lambda t: to_sibling(t).wait_send())
+        unite(TILES - 1)
         for r in range(TILES):
             each(1, n_te, lambda d: p_copy(r, d).wait_send())
 

time: 71.4 us -> 67.7 us (0.948)
  Pallas kernels: 69.7 us -> 65.9 us
    pallas_call x1, Pallas kernels: 69.7 us -> 65.9 us  [on_device(): pl.pallas_call(kernel, out_shape=jax.ShapeDtypeStruct((own, feat), F32),...]
where the time goes in v4:
time: 67.7 us; the launch traced here: 67.5 us
  Pallas kernels  65.9 us (97%)
  local copies, waits for them, and re-layouts  1.59 us (2%)
    pallas_call x1, Pallas kernels, on_device(): pl.pallas_call(kernel, out_shape=jax.ShapeDtypeStruct((own, feat), F32),...  65.9 us
    unnamed x1, local copies, waits for them, and re-layouts  1.59 us

profile of v4, /device:TPU:0, one launch (start us, length us, event | category | flops | bytes accessed | tf_op | source)
XLA Modules:
  0.0 67.5 jit_solution(12313957671050122674)
XLA Ops:
  0.0 65.9 %late_uniting_attention.1 = f32[64,640]{1,0:T(8,128)} custom-call(bf16[64,640]{1,0:T(8,128)(2,1)} %q_hbm.1, bf16[4096,640]{1,0:T(8,128)(2,1)} %k_hbm.1, bf16[4096,640]{1,0:T(8,128)(2,1)} %v_hbm.1, bf16[640,5120]{1,0:T(8,128)(2,1)} %w_hbm.1), custom_call_target="tpu_custom_call" | custom-call | tf_op jit(solution)/shard_map/late_uniting_attention/pallas_call | solution.py:335
  65.9 1.6 %copy.6 = f32[64,640]{1,0:T(8,128)} copy(f32[64,640]{1,0:T(8,128)} %late_uniting_attention.1) | data formatting | bytes 327680

commit v5 on v4

--- a/solution.py
+++ b/solution.py
@@ -269,14 +269,6 @@
             def _():
                 combine(t - LAG)
 
-            for r in range(TILES - 1):
-                @pl.when(t == (r + 1) * heads - 1 + LAG)
-                def _(r=r):
-                    if r == 0:
-                        w_load.wait()
-                    prepare(r)
-                    project(r)
-
         for g in range(len(groups)):
             q_send(g)
         k_load(0).wait()
@@ -303,11 +295,13 @@
         step(last, end[0], None, end[1], None)
         after(last)
         merge(last)
+        w_load.wait()
+        for r in range(TILES - 1):
+            prepare(r)
+            project(r)
         for i in range(LAG - 1, 0, -1):
             combine(last - i)
         prepare(TILES - 1)
-        for r in range(TILES - 1):
-            unite(r)
         combine(last)
         project(TILES - 1)
 
@@ -325,7 +319,8 @@
             else:
                 q_pass(g).wait_send()
         each(0, steps, lambda t: to_sibling(t).wait_send())
-        unite(TILES - 1)
+        for r in range(TILES):
+            unite(r)
         for r in range(TILES):
             each(1, n_te, lambda d: p_copy(r, d).wait_send())
 

time: 67.7 us -> 64.7 us (0.956)
  Pallas kernels: 65.9 us -> 62.9 us
    pallas_call x1, Pallas kernels: 65.9 us -> 62.9 us  [on_device(): pl.pallas_call(kernel, out_shape=jax.ShapeDtypeStruct((own, feat), F32),...]
where the time goes in v5:
time: 64.7 us; the launch traced here: 64.5 us
  Pallas kernels  62.9 us (97%)
  local copies, waits for them, and re-layouts  1.59 us (2%)
    pallas_call x1, Pallas kernels, on_device(): pl.pallas_call(kernel, out_shape=jax.ShapeDtypeStruct((own, feat), F32),...  62.9 us
    unnamed x1, local copies, waits for them, and re-layouts  1.59 us

profile of v5, /device:TPU:0, one launch (start us, length us, event | category | flops | bytes accessed | tf_op | source)
XLA Modules:
  0.0 64.5 jit_solution(5574129686776406669)
XLA Ops:
  0.0 62.9 %late_uniting_attention.1 = f32[64,640]{1,0:T(8,128)} custom-call(bf16[64,640]{1,0:T(8,128)(2,1)} %q_hbm.1, bf16[4096,640]{1,0:T(8,128)(2,1)} %k_hbm.1, bf16[4096,640]{1,0:T(8,128)(2,1)} %v_hbm.1, bf16[640,5120]{1,0:T(8,128)(2,1)} %w_hbm.1), custom_call_target="tpu_custom_call" | custom-call | tf_op jit(solution)/shard_map/late_uniting_attention/pallas_call | solution.py:330
  63.0 1.6 %copy.6 = f32[64,640]{1,0:T(8,128)} copy(f32[64,640]{1,0:T(8,128)} %late_uniting_attention.1) | data formatting | bytes 327680

commit v6 on v5

--- a/solution.py
+++ b/solution.py
@@ -33,8 +33,9 @@
     tile = 2 * half
     steps = TILES * heads
     scale = LOG2E / math.sqrt(HD)
-    groups = [(0, h, h + 1) for h in range(heads)] + [(r, 0, heads) for r in range(1, TILES)]
-    direct = heads
+    groups = [(0, h, h + 1) for h in range(3)] + [(0, 3, heads)] + [(r, 0, heads) for r in range(1, TILES)]
+    relay_at = {g: max(0, r * heads + lo - 3) for g, (r, lo, _) in enumerate(groups)}
+    direct = 3
 
     def kernel(q_hbm, k_hbm, v_hbm, w_hbm, out, qbuf, kbuf, vbuf, wbuf, s_a, s_b, m_a, m_b, keep, give, taken,
                osend, orecv, att, shares, psend, precv,
@@ -257,7 +258,7 @@
 
         def after(t):
             for g in range(direct, len(groups)):
-                @pl.when(t == (groups[g][0] - 1) * heads + 1)
+                @pl.when(t == relay_at[g])
                 def _(g=g):
                     q_relay(g)
 

time: 64.7 us -> 62.7 us (0.969)
  Pallas kernels: 62.9 us -> 61 us
    pallas_call x1, Pallas kernels: 62.9 us -> 61 us  [on_device(): pl.pallas_call(kernel, out_shape=jax.ShapeDtypeStruct((own, feat), F32),...]
where the time goes in v6:
time: 62.7 us; the launch traced here: 62.6 us
  Pallas kernels  61 us (97%)
  local copies, waits for them, and re-layouts  1.59 us (3%)
    pallas_call x1, Pallas kernels, on_device(): pl.pallas_call(kernel, out_shape=jax.ShapeDtypeStruct((own, feat), F32),...  61 us
    unnamed x1, local copies, waits for them, and re-layouts  1.59 us

profile of v6, /device:TPU:0, one launch (start us, length us, event | category | flops | bytes accessed | tf_op | source)
XLA Modules:
  0.0 62.6 jit_solution(15425931614812371612)
XLA Ops:
  0.0 61.0 %late_uniting_attention.1 = f32[64,640]{1,0:T(8,128)} custom-call(bf16[64,640]{1,0:T(8,128)(2,1)} %q_hbm.1, bf16[4096,640]{1,0:T(8,128)(2,1)} %k_hbm.1, bf16[4096,640]{1,0:T(8,128)(2,1)} %v_hbm.1, bf16[640,5120]{1,0:T(8,128)(2,1)} %w_hbm.1), custom_call_target="tpu_custom_call" | custom-call | tf_op jit(solution)/shard_map/late_uniting_attention/pallas_call | solution.py:331
  61.0 1.6 %copy.6 = f32[64,640]{1,0:T(8,128)} copy(f32[64,640]{1,0:T(8,128)} %late_uniting_attention.1) | data formatting | bytes 327680
